TPU v7x, 128 devices: a whole 4x4x4 slice. The times are simulated.
128 devices in a mesh: seq: 8 (over x, core), head: 16 (over z, y).
Axes of the slice: x: 4, y: 4, z: 4, core: 2. Of those that a mesh axis runs over, the one named last changes fastest.
Arguments:
- tokens: bfloat16 [1024, 6144], P('seq'), may hold values from -6 to 6
- log_decay: float32 [1024, 32], P('seq', 'head'), may hold values from -1 to 0
- carried_state: float32 [32, 128, 128], P('head'), may hold values from -48 to 48
- q_weight: bfloat16 [6144, 4096], P(None, 'head'), may hold values from -0.078125 to 0.078125
- k_weight: bfloat16 [6144, 4096], P(None, 'head'), may hold values from -0.078125 to 0.078125
- v_weight: bfloat16 [6144, 4096], P(None, 'head'), may hold values from -0.078125 to 0.078125
- out_weight: bfloat16 [4096, 6144], P('head'), may hold values from -0.09375 to 0.09375
- final_gain: bfloat16 [6144], replicated, may hold values from 0.099609375 to 1.8984375
- vocab_weight: bfloat16 [6144, 131072], P(None, ('seq', 'head')), may hold values from -5 to 5
- targets: int32 [1024], replicated, may hold values from 0 to 131071
Outputs:
- loglik: float32 [1024], P('seq')
All inputs are finite; a program needn't handle non-finite values.
Results may differ from a plain program's by a relative error of at most 0.002.
Values may be sent and summed in bfloat16 or wider, within the bound.
No kernel may reach another device: no remote copies, remote signals or barrier semaphores. Data moves between devices by JAX's collectives and lax.ppermute only.
A program may use at most 128 MiB of HBM per device.

v0:
```python
import jax
import jax.numpy as jnp
from jax import lax
from jax.sharding import PartitionSpec as P


def prefix(array, axis, combine, identity):
    length, here = (lax.axis_size(axis), lax.axis_index(axis))
    everything = jax.tree.map(lambda part: lax.all_gather(part, axis), array)
    start = jax.tree.map(
        lambda part, zero: jnp.broadcast_to(jnp.asarray(zero, part.dtype), part.shape),
        array,
        identity,
    )

    def turn(k, before):
        reached = k < here
        new = combine(before, jax.tree.map(lambda part: part[k], everything))
        return jax.tree.map(lambda a, b: jnp.where(reached, a, b), new, before)

    return lax.fori_loop(0, length, turn, start)


def combine_states(earlier, later):
    return (earlier[0] * later[0], later[0][:, None, None] * earlier[1] + later[1])


def shards(
    tokens,
    log_decay,
    carried_state,
    q_weight,
    k_weight,
    v_weight,
    out_weight,
    final_gain,
    vocab_weight,
    targets,
):
    highest = lax.Precision.HIGHEST
    rows_here = tokens.shape[0]
    heads_here = carried_state.shape[0]
    head_size = carried_state.shape[1]
    view = (rows_here, heads_here, head_size)
    queries = (
        jnp.dot(tokens, q_weight, preferred_element_type=jnp.float32)
        .astype(jnp.bfloat16)
        .reshape(view)
    )
    keys_loc = (
        jnp.dot(tokens, k_weight, preferred_element_type=jnp.float32)
        .astype(jnp.bfloat16)
        .reshape(view)
    )
    values = (
        jnp.dot(tokens, v_weight, preferred_element_type=jnp.float32)
        .astype(jnp.bfloat16)
        .reshape(view)
    )
    cumul = jnp.cumsum(log_decay, axis=0)
    last_cum = cumul[-1]
    ends = jnp.exp(last_cum[None, :] - cumul)
    local_state = jnp.einsum(
        "thd,the->hde",
        keys_loc.astype(jnp.float32) * ends[:, :, None],
        values.astype(jnp.float32),
        precision=highest,
    )
    total_decay = jnp.exp(last_cum)
    prefix_decay, prefix_state = prefix(
        (total_decay, local_state),
        "seq",
        combine_states,
        (jnp.ones_like(total_decay), jnp.zeros_like(local_state)),
    )
    lower = jnp.arange(rows_here)[:, None] >= jnp.arange(rows_here)[None, :]
    scores = jnp.einsum("thd,shd->hts", queries, keys_loc, preferred_element_type=jnp.float32)
    diff = jnp.transpose(cumul[:, None, :] - cumul[None, :, :], (2, 0, 1))
    weight = (scores * jnp.exp(jnp.where(lower[None], diff, -1e30))).astype(jnp.bfloat16)
    intra = jnp.einsum("hts,shd->thd", weight, values, preferred_element_type=jnp.float32)
    state_in = prefix_decay[:, None, None] * carried_state + prefix_state
    inter = jnp.exp(cumul)[:, :, None] * jnp.einsum(
        "thd,hde->the", queries.astype(jnp.float32), state_in, precision=highest
    )
    attended = intra + inter
    normed_heads = attended * lax.rsqrt(
        jnp.mean(attended * attended, axis=-1, keepdims=True) + 1e-06
    )
    flat_heads = normed_heads.astype(jnp.bfloat16).reshape(rows_here, heads_here * head_size)
    rows_mine = rows_here // lax.axis_size("head")
    head_index = lax.axis_index("head")
    mixed_all = lax.psum(
        jnp.dot(flat_heads, out_weight, preferred_element_type=jnp.float32), "head"
    )
    mixed = lax.dynamic_slice_in_dim(mixed_all, head_index * rows_mine, rows_mine, 0)
    resid = (
        lax.dynamic_slice_in_dim(tokens, head_index * rows_mine, rows_mine, 0).astype(jnp.float32)
        + mixed
    )
    final_rows = (
        resid
        * lax.rsqrt(jnp.mean(resid * resid, axis=-1, keepdims=True) + 1e-06)
        * final_gain.astype(jnp.float32)
    )
    final_rows = final_rows.astype(jnp.bfloat16)
    vocab_local = vocab_weight.shape[1]
    offset = (lax.axis_index("seq") * lax.axis_size("head") + head_index) * vocab_local
    columns = jnp.arange(vocab_local, dtype=jnp.int32)
    logits = jnp.dot(
        lax.all_gather(final_rows, ("seq", "head"), axis=0, tiled=True),
        vocab_weight,
        preferred_element_type=jnp.float32,
    )
    top = jnp.max(logits, axis=1)
    total = jnp.sum(jnp.exp(logits - top[:, None]), axis=1)
    wanted = targets - offset
    hit = jnp.sum(jnp.where(columns[None, :] == wanted[:, None], logits, 0.0), axis=1)
    top_all = lax.pmax(top, ("seq", "head"))
    total_all, hit_all = lax.psum((total * jnp.exp(top - top_all), hit), ("seq", "head"))
    loglik = hit_all - top_all - jnp.log(total_all)
    return lax.dynamic_slice_in_dim(loglik, lax.axis_index("seq") * rows_here, rows_here, 0)


def solution(mesh):
    return jax.shard_map(
        shards,
        mesh=mesh,
        in_specs=(
            P("seq", None),
            P("seq", "head"),
            P("head", None, None),
            P(None, "head"),
            P(None, "head"),
            P(None, "head"),
            P("head", None),
            P(),
            P(None, ("seq", "head")),
            P(),
        ),
        out_specs=P("seq"),
        check_vma=False,
    )
```

profile of v0, /device:TPU:1, one launch (start us, length us, event | category | flops | bytes accessed | tf_op | source)
XLA Modules:
  0.0 385.3 jit_solution(14718534888018662489)
XLA Ops:
  6.5 0.0 copy-start
  6.5 0.0 all-gather.7.cloned.1.call-start
  6.5 0.9 copy.23
  7.5 0.2 reduce_window_sum.11
  7.7 0.1 copy.30
  7.7 3.0 convolution_convert_fusion
  10.7 0.1 copy.36
  10.8 3.0 fusion.4
  13.8 0.9 fusion.8
  14.6 0.0 all-gather.7.cloned.1.call-update
  14.7 0.0 all-reduce.3.cloned.1.call-start
  14.7 11.8 %all-gather.1 = f32[8,1,2]{2,1,0:T(1,128)S(1)} all-gather(f32[1,1,2]{2,1,0:T(1,128)S(1)} %get-tuple-element.171), channel_id=1, replica_groups=mesh['seq'=8,'head'=16] {'seq'}, dimensions={0}, use_global_device_ids=true | all-gather | bytes 72 | tf_op jit(solution)/shard_map/all_gather | solution.py:9
  26.5 0.1 copy.27
  26.6 0.1 copy.24
  26.7 3.1 fusion.5
  29.8 12.0 %all-gather.7.cloned.1.call-done = f32[16,128,128]{2,1,0:T(8,128)} async-done(((f32[2,128,128]{2,1,0:T(8,128)}), f32[16,128,128]{2,1,0:T(8,128)}) %all-gather.7.cloned.1.call-update) | async-done | bytes 1048592 | tf_op jit(solution)/shard_map/all_gather | solution.py:9
  41.8 8.3 %while.16 = (s32[]{:T(128)}, f32[2]{0:T(128)S(1)}, f32[2,128,128]{2,1,0:T(8,128)S(1)}, s32[]{:T(128)}, f32[8,2]{1,0:T(8,128)S(1)}, /*index=5*/f32[8,2,128,128]{3,2,1,0:T(8,128)}, s32[]{:T(128)}, s32[]{:T(128)}) while((s32[]{:T(128)}, f32[2]{0:T(128)S(1)}, f32[2,128,128]{2,1,0:T(8,128)S(1)}, s32[]{:T(128)}, f32[8,2]{1,0:T(8,128)S(1)}, ...), condition=%wide.region_2.3_spmd.clone, body=%wide.region_1.2_spmd.clone.sunk | while | flops 131082 | bytes 393371 | solution.py:21
  41.8 1.0 fusion.48
  42.8 1.0 fusion.48
  43.9 1.0 fusion.48
  44.9 1.0 fusion.48
  46.0 1.0 fusion.48
  47.0 1.0 fusion.48
  48.0 1.0 fusion.48
  49.1 1.0 fusion.48
  50.1 1.9 fusion.1
  52.0 1.2 multiply_reduce_fusion.1
  53.3 0.0 copy-done
  53.3 2.3 fusion.35
  55.6 0.0 copy-start.1
  55.6 0.0 copy-start.2
  55.6 0.0 all-reduce.3.cloned.1.call-update
  55.6 0.0 all-gather.5.cloned.1.call-start
  55.7 0.6 copy-done.1
  56.3 94.3 %all-reduce.3.cloned.1.call-done = f32[128,6144]{1,0:T(8,128)} async-done(((f32[128,6144]{1,0:T(8,128)}), f32[128,6144]{1,0:T(8,128)}) %all-reduce.3.cloned.1.call-update) | async-done | bytes 3145744 | tf_op jit(solution)/shard_map/psum | solution.py:92
  150.6 1.2 multiply_reduce_fusion
  151.8 1.7 multiply_convert_fusion
  153.5 0.0 all-gather.5.cloned.1.call-update
  153.5 0.0 copy-done.2
  153.6 73.3 %all-gather.5.cloned.1.call-done = bf16[1024,6144]{1,0:T(8,128)(2,1)} async-done(((bf16[8,6144]{1,0:T(8,128)(2,1)}), bf16[1024,6144]{1,0:T(8,128)(2,1)}) %all-gather.5.cloned.1.call-update) | async-done | bytes 12582928 | tf_op jit(solution)/shard_map/all_gather | solution.py:110
  226.9 19.4 %fusion.34 = (f32[1024]{0:T(1024)S(1)}, f32[1024,1024]{0,1:T(8,128)}) fusion(bf16[1024,6144]{1,0:T(8,128)(2,1)} %all-gather.5.cloned.1.call-done, bf16[6144,1024]{1,0:T(8,128)(2,1)} %param.20), kind=kOutput, calls=%fused_computation.57 | convolution fusion | flops 12885949440 | bytes 29364224 | tf_op jit(solution)/shard_map/dot_general | solution.py:109
  246.3 64.4 %pmax.7 = f32[1024]{0:T(1024)S(1)} all-reduce(f32[1024]{0:T(1024)S(1)} %get-tuple-element.174), channel_id=1, replica_groups=mesh['seq'=8,'head'=16] {'seq','head'}, use_global_device_ids=true, to_apply=%region_9.10 | all-reduce | flops 1024 | bytes 8192 | tf_op jit(solution)/shard_map/pmax | solution.py:118
  310.7 3.3 select_reduce_fusion
  314.0 64.2 %all-reduce = (f32[1024]{0:T(1024)S(1)}, f32[1024]{0:T(1024)S(1)}) all-reduce(f32[1024]{0:T(1024)S(1)} %exponential_multiply_fusion, f32[1024]{0:T(1024)S(1)} %get-tuple-element.150), channel_id=1, replica_groups=mesh['seq'=8,'head'=16] {'seq','head'}, use_global_device_ids=true, to_apply=%region_11.12 | all-reduce | flops 2048 | bytes 16384 | tf_op jit(solution)/shard_map/psum | solution.py:119
  378.2 0.6 dynamic_slice.25
  (20 shorter events, 0.3 us)
Async XLA Ops:
  6.5 46.7 %copy-start = (bf16[256,6144]{1,0:T(8,128)(2,1)S(1)}, bf16[256,6144]{1,0:T(8,128)(2,1)}, u32[]{:S(2)}) copy-start(bf16[256,6144]{1,0:T(8,128)(2,1)} %param.18) | copy-start | bytes 9437188
  6.5 35.2 %all-gather.7.cloned.1.call-start = ((), (), s32[]{:S(2)}) async-start(), calls=%async_computation.2 | async-start | bytes 1179648 | tf_op jit(solution)/shard_map/all_gather | solution.py:9
  14.7 135.9 %all-reduce.3.cloned.1.call-start = ((), (), s32[]{:S(2)}) async-start(), calls=%async_computation | async-start | bytes 6291456 | tf_op jit(solution)/shard_map/psum | solution.py:92
  55.6 0.7 copy-start.1
  55.6 98.0 %copy-start.2 = (s32[1024]{0:T(1024)S(1)}, s32[1024]{0:T(1024)}, u32[]{:S(2)}) copy-start(s32[1024]{0:T(1024)} %param.21) | copy-start | bytes 12292
  55.6 171.3 %all-gather.5.cloned.1.call-start = ((), (), s32[]{:S(2)}) async-start(), calls=%async_computation.1 | async-start | bytes 12681216 | tf_op jit(solution)/shard_map/all_gather | solution.py:110
Sparse Core Ops, SparseCore 0:
  14.8 26.9 all-gather.6
  55.7 94.8 all-reduce.2
  153.7 73.0 all-gather.4
where the time goes:
time: 386 us; the launch traced here: 385 us
  waiting for transfers between devices  180 us (47%)
  blocking collectives  140 us (36%)
  matrix products  34.7 us (9%)
  other arithmetic  14.5 us (4%)
  between operations  13.2 us (3%)
    psum x1, waiting for transfers between devices, shards(): lax.psum(jnp.dot(flat_heads, out_weight, preferred_element_type=jnp.float...  94.3 us
    all_gather x1, waiting for transfers between devices, shards(): lax.all_gather(final_rows, ('seq', 'head'), axis=0, tiled=True)  73.3 us
    pmax x1, blocking collectives, shards(): top_all = lax.pmax(top, ('seq', 'head'))  64.4 us
    psum x1, blocking collectives, shards(): lax.psum((total * jnp.exp(top - top_all), hit), ('seq', 'head'))  64.2 us
    dot_general x1, matrix products, shards(): jnp.dot(lax.all_gather(final_rows, ('seq', 'head'), axis=0, tiled=True),...  19.4 us
    all_gather x1, waiting for transfers between devices, prefix(): everything = jax.tree.map(lambda part: lax.all_gather(part, axis), array)  12 us
    all_gather x1, blocking collectives, prefix(): everything = jax.tree.map(lambda part: lax.all_gather(part, axis), array)  11.8 us
    select_n x16, other arithmetic, turn(): return jax.tree.map(lambda a, b: jnp.where(reached, a, b), new, before)  8.09 us
  transfers between devices with their start and end apart: 3, of which 3 were waited for; matrix products, arithmetic and copies ran while one was open for 1% of the time, Pallas kernels for 0%

commit v1 on v0

--- a/solution.py
+++ b/solution.py
@@ -2,6 +2,12 @@
 import jax.numpy as jnp
 from jax import lax
 from jax.sharding import PartitionSpec as P
+
+
+def place_steps_all(sample, mesh_ax, which_axis):
+    for k0 in (mesh_ax, which_axis):
+        sample = lax.psum(sample, axis_name=k0)
+    return sample
 
 
 def prefix(array, axis, combine, identity):
@@ -116,7 +122,7 @@
     wanted = targets - offset
     hit = jnp.sum(jnp.where(columns[None, :] == wanted[:, None], logits, 0.0), axis=1)
     top_all = lax.pmax(top, ("seq", "head"))
-    total_all, hit_all = lax.psum((total * jnp.exp(top - top_all), hit), ("seq", "head"))
+    total_all, hit_all = place_steps_all((total * jnp.exp(top - top_all), hit), "head", "seq")
     loglik = hit_all - top_all - jnp.log(total_all)
     return lax.dynamic_slice_in_dim(loglik, lax.axis_index("seq") * rows_here, rows_here, 0)
 

time: 386 us -> 373 us (0.966)
  blocking collectives: 140 us -> 128 us
    psum x1 -> x2, blocking collectives: 64.2 us -> 51.3 us  [place_steps_all(): sample = lax.psum(sample, axis_name=k0)]
where the time goes in v1:
time: 373 us; the launch traced here: 372 us
  waiting for transfers between devices  180 us (48%)
  blocking collectives  128 us (34%)
  matrix products  34.7 us (9%)
  other arithmetic  14.5 us (4%)
  between operations  13.3 us (4%)
    psum x1, waiting for transfers between devices, shards(): lax.psum(jnp.dot(flat_heads, out_weight, preferred_element_type=jnp.float...  94.3 us
    all_gather x1, waiting for transfers between devices, shards(): lax.all_gather(final_rows, ('seq', 'head'), axis=0, tiled=True)  73.3 us
    pmax x1, blocking collectives, shards(): top_all = lax.pmax(top, ('seq', 'head'))  64.4 us
    psum x2, blocking collectives, place_steps_all(): sample = lax.psum(sample, axis_name=k0)  51.3 us
    dot_general x1, matrix products, shards(): jnp.dot(lax.all_gather(final_rows, ('seq', 'head'), axis=0, tiled=True),...  19.4 us
    all_gather x1, waiting for transfers between devices, prefix(): everything = jax.tree.map(lambda part: lax.all_gather(part, axis), array)  12 us
    all_gather x1, blocking collectives, prefix(): everything = jax.tree.map(lambda part: lax.all_gather(part, axis), array)  11.8 us
    select_n x16, other arithmetic, turn(): return jax.tree.map(lambda a, b: jnp.where(reached, a, b), new, before)  8.09 us
  transfers between devices with their start and end apart: 3, of which 3 were waited for; matrix products, arithmetic and copies ran while one was open for 1% of the time, Pallas kernels for 0%

profile of v1, /device:TPU:1, one launch (start us, length us, event | category | flops | bytes accessed | tf_op | source)
XLA Modules:
  0.0 372.4 jit_solution(12365409129073786822)
XLA Ops:
  6.5 0.0 copy-start
  6.5 0.0 all-gather.7.cloned.1.call-start
  6.5 0.9 copy.23
  7.5 0.2 reduce_window_sum.11
  7.7 0.1 copy.30
  7.7 3.0 convolution_convert_fusion
  10.7 0.1 copy.36
  10.8 3.0 fusion.4
  13.8 0.9 fusion.8
  14.6 0.0 all-gather.7.cloned.1.call-update
  14.7 0.0 all-reduce.4.cloned.1.call-start
  14.7 11.8 %all-gather.1 = f32[8,1,2]{2,1,0:T(1,128)S(1)} all-gather(f32[1,1,2]{2,1,0:T(1,128)S(1)} %get-tuple-element.173), channel_id=1, replica_groups=mesh['seq'=8,'head'=16] {'seq'}, dimensions={0}, use_global_device_ids=true | all-gather | bytes 72 | tf_op jit(solution)/shard_map/all_gather | solution.py:15
  26.5 0.1 copy.27
  26.6 0.1 copy.24
  26.7 3.1 fusion.5
  29.8 12.0 %all-gather.7.cloned.1.call-done = f32[16,128,128]{2,1,0:T(8,128)} async-done(((f32[2,128,128]{2,1,0:T(8,128)}), f32[16,128,128]{2,1,0:T(8,128)}) %all-gather.7.cloned.1.call-update) | async-done | bytes 1048592 | tf_op jit(solution)/shard_map/all_gather | solution.py:15
  41.8 8.3 %while.16 = (s32[]{:T(128)}, f32[2]{0:T(128)S(1)}, f32[2,128,128]{2,1,0:T(8,128)S(1)}, s32[]{:T(128)}, f32[8,2]{1,0:T(8,128)S(1)}, /*index=5*/f32[8,2,128,128]{3,2,1,0:T(8,128)}, s32[]{:T(128)}, s32[]{:T(128)}) while((s32[]{:T(128)}, f32[2]{0:T(128)S(1)}, f32[2,128,128]{2,1,0:T(8,128)S(1)}, s32[]{:T(128)}, f32[8,2]{1,0:T(8,128)S(1)}, ...), condition=%wide.region_2.3_spmd.clone, body=%wide.region_1.2_spmd.clone.sunk | while | flops 131082 | bytes 393371 | solution.py:27
  41.8 1.0 fusion.48
  42.8 1.0 fusion.48
  43.9 1.0 fusion.48
  44.9 1.0 fusion.48
  46.0 1.0 fusion.48
  47.0 1.0 fusion.48
  48.0 1.0 fusion.48
  49.1 1.0 fusion.48
  50.1 1.9 fusion.1
  52.0 1.2 multiply_reduce_fusion.1
  53.3 0.0 copy-done
  53.3 2.3 fusion.35
  55.6 0.0 copy-start.1
  55.6 0.0 copy-start.2
  55.6 0.0 all-reduce.4.cloned.1.call-update
  55.6 0.0 all-gather.5.cloned.1.call-start
  55.7 0.6 copy-done.1
  56.3 94.3 %all-reduce.4.cloned.1.call-done = f32[128,6144]{1,0:T(8,128)} async-done(((f32[128,6144]{1,0:T(8,128)}), f32[128,6144]{1,0:T(8,128)}) %all-reduce.4.cloned.1.call-update) | async-done | bytes 3145744 | tf_op jit(solution)/shard_map/psum | solution.py:98
  150.6 1.2 multiply_reduce_fusion
  151.8 1.7 multiply_convert_fusion
  153.5 0.0 all-gather.5.cloned.1.call-update
  153.5 0.0 copy-done.2
  153.6 73.3 %all-gather.5.cloned.1.call-done = bf16[1024,6144]{1,0:T(8,128)(2,1)} async-done(((bf16[8,6144]{1,0:T(8,128)(2,1)}), bf16[1024,6144]{1,0:T(8,128)(2,1)}) %all-gather.5.cloned.1.call-update) | async-done | bytes 12582928 | tf_op jit(solution)/shard_map/all_gather | solution.py:116
  226.9 19.4 %fusion.34 = (f32[1024]{0:T(1024)S(1)}, f32[1024,1024]{0,1:T(8,128)}) fusion(bf16[1024,6144]{1,0:T(8,128)(2,1)} %all-gather.5.cloned.1.call-done, bf16[6144,1024]{1,0:T(8,128)(2,1)} %param.20), kind=kOutput, calls=%fused_computation.57 | convolution fusion | flops 12885949440 | bytes 29364224 | tf_op jit(solution)/shard_map/dot_general | solution.py:115
  246.3 64.4 %pmax.7 = f32[1024]{0:T(1024)S(1)} all-reduce(f32[1024]{0:T(1024)S(1)} %get-tuple-element.176), channel_id=1, replica_groups=mesh['seq'=8,'head'=16] {'seq','head'}, use_global_device_ids=true, to_apply=%region_10.11 | all-reduce | flops 1024 | bytes 8192 | tf_op jit(solution)/shard_map/pmax | solution.py:124
  310.7 3.3 select_reduce_fusion
  314.0 31.3 %all-reduce = (f32[1024]{0:T(1024)S(1)}, f32[1024]{0:T(1024)S(1)}) all-reduce(f32[1024]{0:T(1024)S(1)} %exponential_multiply_fusion, f32[1024]{0:T(1024)S(1)} %get-tuple-element.150), channel_id=1, replica_groups=mesh['seq'=8,'head'=16] {'head'}, use_global_device_ids=true, to_apply=%region_12.13 | all-reduce | flops 2048 | bytes 16384 | tf_op jit(solution)/shard_map/psum | solution.py:9
  345.3 20.0 %all-reduce.1 = (f32[1024]{0:T(1024)S(1)}, f32[1024]{0:T(1024)S(1)}) all-reduce(f32[1024]{0:T(1024)S(1)} %get-tuple-element.164, f32[1024]{0:T(1024)S(1)} %get-tuple-element.165), channel_id=1, replica_groups=mesh['seq'=8,'head'=16] {'seq'}, use_global_device_ids=true, to_apply=%region_13.14 | all-reduce | flops 2048 | bytes 16384 | tf_op jit(solution)/shard_map/psum | solution.py:9
  365.3 0.6 dynamic_slice.25
  (20 shorter events, 0.3 us)
Async XLA Ops:
  6.5 46.7 %copy-start = (bf16[256,6144]{1,0:T(8,128)(2,1)S(1)}, bf16[256,6144]{1,0:T(8,128)(2,1)}, u32[]{:S(2)}) copy-start(bf16[256,6144]{1,0:T(8,128)(2,1)} %param.18) | copy-start | bytes 9437188
  6.5 35.2 %all-gather.7.cloned.1.call-start = ((), (), s32[]{:S(2)}) async-start(), calls=%async_computation.2 | async-start | bytes 1179648 | tf_op jit(solution)/shard_map/all_gather | solution.py:15
  14.7 135.9 %all-reduce.4.cloned.1.call-start = ((), (), s32[]{:S(2)}) async-start(), calls=%async_computation | async-start | bytes 6291456 | tf_op jit(solution)/shard_map/psum | solution.py:98
  55.6 0.7 copy-start.1
  55.6 98.0 %copy-start.2 = (s32[1024]{0:T(1024)S(1)}, s32[1024]{0:T(1024)}, u32[]{:S(2)}) copy-start(s32[1024]{0:T(1024)} %param.21) | copy-start | bytes 12292
  55.6 171.3 %all-gather.5.cloned.1.call-start = ((), (), s32[]{:S(2)}) async-start(), calls=%async_computation.1 | async-start | bytes 12681216 | tf_op jit(solution)/shard_map/all_gather | solution.py:116
Sparse Core Ops, SparseCore 0:
  14.8 26.9 all-gather.6
  55.7 94.8 all-reduce.3
  153.7 73.0 all-gather.4
